TPU v7x, 32 devices: a whole 2x2x4 slice. The times are simulated.
32 devices in a mesh: batch: 2 (over core), lon: 4 (over y, x), lat: 4 (over z).
Axes of the slice: x: 2, y: 2, z: 4, core: 2. Of those that a mesh axis runs over, the one named last changes fastest.
Arguments:
- imagery: bfloat16 [6, 512, 4096], P('batch', 'lat', 'lon'), parts along dimension 0, may hold values from -6 to 6
- stem_weight: bfloat16 [4, 768, 1024], replicated, may hold values from -0.109375 to 0.109375
- down_weight: bfloat16 [1024, 512], replicated, may hold values from -0.1875 to 0.1875
- height_qkv: bfloat16 [512, 1024], replicated, may hold values from -0.25 to 0.25
- height_bias: float32 [8, 63], replicated, may hold values from -1.5 to 301.5
- width_qkv: bfloat16 [512, 1024], replicated, may hold values from -0.25 to 0.25
- width_bias: float32 [8, 256], replicated, may hold values from -1.5 to 301.5
- up_weight: bfloat16 [512, 1024], replicated, may hold values from -0.25 to 0.25
Outputs:
- block_output: bfloat16 [64, 256, 1024], P(('batch', 'lat'), 'lon'), parts along dimension 0
There are 2 independent parts, one for each index of `batch`. A program takes and returns all parts, laid end to end along the dimension named above; an argument that names none is the same for every part. Nothing has to cross between parts.
All inputs are finite; a program needn't handle non-finite values.
Results may differ from a plain program's by a relative error of at most 0.012.
Values may be sent and summed in bfloat16 or wider, within the bound.
A program may use at most 128 MiB of HBM per device.

v0:
```python
import jax
import jax.numpy as jnp
from jax import lax
from jax.sharding import PartitionSpec as P

QK = 256
VD = 512
HEADS = 8
PATCH = 16
DQ = 32
DV = 64
lowest_score = -1e30


def extended(cells, sides, width, closed):
    for axis, dim in sides:
        count = lax.axis_size(axis)
        ends = count if closed else count - 1
        head = lax.slice_in_dim(cells, 0, width, axis=dim)
        tail = lax.slice_in_dim(cells, cells.shape[dim] - width, cells.shape[dim], axis=dim)
        cells = jnp.concatenate(
            [
                lax.ppermute(tail, axis, [(i, (i + 1) % count) for i in range(ends)]),
                cells,
                lax.ppermute(head, axis, [((i + 1) % count, i) for i in range(ends)]),
            ],
            axis=dim,
        )
    return cells


def stem_features(padded, stem_weight, map_rows, map_cols):
    channels = padded.shape[0]
    blocks = padded.reshape(channels, map_rows + 1, PATCH, map_cols + 1, PATCH)
    blocks = blocks.transpose(1, 3, 0, 2, 4).reshape(
        map_rows + 1, map_cols + 1, channels * PATCH * PATCH
    )
    summed = jnp.zeros((map_rows * map_cols, stem_weight.shape[2]), jnp.float32)
    for row_shift in range(2):
        for col_shift in range(2):
            window = blocks[row_shift : row_shift + map_rows, col_shift : col_shift + map_cols]
            window = window.reshape(map_rows * map_cols, channels * PATCH * PATCH)
            summed = summed + jnp.dot(
                window, stem_weight[2 * row_shift + col_shift], preferred_element_type=jnp.float32
            )
    return jax.nn.relu(summed).astype(jnp.bfloat16)


def online_update(carried, scores, value_heads, form):
    running_max, denominator, weighted = carried
    new_peak = jnp.maximum(running_max, jnp.max(scores, axis=-1))
    weights = jnp.exp(scores - new_peak[..., None])
    denominator = jnp.sum(weights, axis=-1)
    weighted = jnp.einsum(
        form, weights.astype(jnp.bfloat16), value_heads, preferred_element_type=jnp.float32
    )
    return (new_peak, denominator, weighted)


def on_device(
    imagery, stem_weight, down_weight, height_qkv, height_bias, width_qkv, width_bias, up_weight
):
    rim_width = PATCH // 2
    widened = extended(imagery, (("lon", 2),), rim_width, True)
    padded = extended(widened, (("lat", 1),), rim_width, False)
    map_rows = imagery.shape[1] // PATCH
    map_cols = imagery.shape[2] // PATCH
    full_height = map_rows * lax.axis_size("lat")
    full_width = map_cols * lax.axis_size("lon")
    row_first = lax.axis_index("lat") * map_rows
    col_first = lax.axis_index("lon") * map_cols
    score_scale = DQ ** (-0.5)
    features = stem_features(padded, stem_weight, map_rows, map_cols)
    middle = jax.nn.relu(jnp.dot(features, down_weight, preferred_element_type=jnp.float32)).astype(
        jnp.bfloat16
    )
    height_proj = jnp.dot(middle, height_qkv, preferred_element_type=jnp.float32).astype(
        jnp.bfloat16
    )
    height_proj = height_proj.reshape(map_rows, map_cols, 2 * QK + VD)
    height_queries = height_proj[..., :QK].reshape(map_rows, map_cols, HEADS, DQ)
    initial = (
        jnp.full((HEADS, map_cols, map_rows), lowest_score, jnp.float32),
        jnp.zeros((HEADS, map_cols, map_rows), jnp.float32),
        jnp.zeros((HEADS, map_cols, map_rows, DV), jnp.float32),
    )
    key_rows = lax.all_gather(height_proj[..., QK : 2 * QK], "lat", axis=0, tiled=True)
    value_rows = lax.all_gather(height_proj[..., 2 * QK :], "lat", axis=0, tiled=True)
    key_count = key_rows.shape[0]
    scores = (
        jnp.einsum(
            "pwnd,ownd->nwpo",
            height_queries,
            key_rows.reshape(key_count, map_cols, HEADS, DQ),
            preferred_element_type=jnp.float32,
        )
        * score_scale
    )
    offsets = (
        jnp.arange(key_count, dtype=jnp.int32)[None, :]
        - (row_first + jnp.arange(map_rows, dtype=jnp.int32))[:, None]
        + full_height
        - 1
    )
    scores = scores + jnp.take(height_bias, offsets, axis=1)[:, None]
    running_max, denominator, weighted = online_update(
        initial, scores, value_rows.reshape(key_count, map_cols, HEADS, DV), "nwpo,ownd->nwpd"
    )
    height_out = (
        (weighted / denominator[..., None])
        .transpose(2, 1, 0, 3)
        .reshape(map_rows, map_cols, VD)
        .astype(jnp.bfloat16)
    )
    width_proj = jnp.dot(
        height_out.reshape(map_rows * map_cols, VD), width_qkv, preferred_element_type=jnp.float32
    ).astype(jnp.bfloat16)
    width_proj = width_proj.reshape(map_rows, map_cols, 2 * QK + VD)
    width_queries = width_proj[..., :QK].reshape(map_rows, map_cols, HEADS, DQ)
    width_initial = (
        jnp.full((HEADS, map_rows, map_cols), lowest_score, jnp.float32),
        jnp.zeros((HEADS, map_rows, map_cols), jnp.float32),
        jnp.zeros((HEADS, map_rows, map_cols, DV), jnp.float32),
    )
    key_cols = lax.all_gather(width_proj[..., QK : 2 * QK], "lon", axis=1, tiled=True)
    value_cols = lax.all_gather(width_proj[..., 2 * QK :], "lon", axis=1, tiled=True)
    key_count = key_cols.shape[1]
    scores = (
        jnp.einsum(
            "hwnd,hknd->nhwk",
            width_queries,
            key_cols.reshape(map_rows, key_count, HEADS, DQ),
            preferred_element_type=jnp.float32,
        )
        * score_scale
    )
    offsets = (
        jnp.arange(key_count, dtype=jnp.int32)[None, :]
        - (col_first + jnp.arange(map_cols, dtype=jnp.int32))[:, None]
    ) % full_width
    scores = scores + jnp.take(width_bias, offsets, axis=1)[:, None]
    width_max, width_denominator, width_weighted = online_update(
        width_initial, scores, value_cols.reshape(map_rows, key_count, HEADS, DV), "nhwk,hknd->nhwd"
    )
    width_out = (
        (width_weighted / width_denominator[..., None])
        .transpose(1, 2, 0, 3)
        .reshape(map_rows * map_cols, VD)
        .astype(jnp.bfloat16)
    )
    branch = jnp.dot(jax.nn.relu(width_out), up_weight, preferred_element_type=jnp.float32)
    result = jax.nn.relu(features.astype(jnp.float32) + branch).astype(jnp.bfloat16)
    return result.reshape(map_rows, map_cols, up_weight.shape[1])


def solution(mesh):
    placed = (P("batch", "lat", "lon"), P(), P(), P(), P(), P(), P(), P())
    return jax.shard_map(
        on_device,
        mesh=mesh,
        in_specs=placed,
        out_specs=P(("batch", "lat"), "lon", None),
        check_vma=False,
    )
```

profile of v0, /device:TPU:0, one launch (start us, length us, event | category | flops | bytes accessed | tf_op | source)
XLA Modules:
  0.0 249.6 jit_solution(9862370127342275498)
XLA Ops:
  6.5 1.1 fusion.62
  7.7 3.0 %collective-permute-start = (bf16[3,128,8]{2,1,0:T(8,128)(2,1)S(1)}, bf16[3,128,8]{2,1,0:T(8,128)(2,1)S(1)}, u32[]{:S(2)}, u32[]{:S(2)}) collective-permute-start(bf16[3,128,8]{2,1,0:T(8,128)(2,1)S(1)} %get-tuple-element.16), channel_id=1, source_target_pairs={{0,4},{4,8},{8,12},{12,0},{1,5},{5,9},{9,13},{13,1},{2,6},{6,10},{... | collective-permute-start | bytes 18440 | tf_op jit(solution)/shard_map/ppermute | solution.py:23
  10.7 1.0 collective-permute-start.1
  11.7 3.4 %collective-permute-done = bf16[3,128,8]{2,1,0:T(8,128)(2,1)S(1)} collective-permute-done((bf16[3,128,8]{2,1,0:T(8,128)(2,1)S(1)}, bf16[3,128,8]{2,1,0:T(8,128)(2,1)S(1)}, u32[]{:S(2)}, u32[]{:S(2)}) %collective-permute-start) | collective-permute-done | bytes 6176 | tf_op jit(solution)/shard_map/ppermute | solution.py:23
  15.1 1.7 collective-permute-done.1
  16.8 1.8 concatenate.6
  18.6 3.5 %collective-permute-start.2 = (bf16[3,8,1040]{2,1,0:T(8,128)(2,1)S(1)}, bf16[3,8,1040]{2,1,0:T(8,128)(2,1)S(1)}, u32[]{:S(2)}, u32[]{:S(2)}) collective-permute-start(bf16[3,8,1040]{2,1,0:T(8,128)(2,1)S(1)} %get-tuple-element.13), channel_id=1, source_target_pairs={{0,1},{1,2},{2,3},{4,5},{5,6},{6,7},{8,9},{9,10},{10,11},{12,13},{... | collective-permute-start | bytes 149768 | tf_op jit(solution)/shard_map/ppermute | solution.py:23
  22.1 1.3 collective-permute-start.3
  23.9 4.3 %collective-permute-done.3 = bf16[3,8,1040]{2,1,0:T(8,128)(2,1)S(1)} collective-permute-done((bf16[3,8,1040]{2,1,0:T(8,128)(2,1)S(1)}, bf16[3,8,1040]{2,1,0:T(8,128)(2,1)S(1)}, u32[]{:S(2)}, u32[]{:S(2)}) %collective-permute-start.3) | collective-permute-done | bytes 49952 | tf_op jit(solution)/shard_map/ppermute | solution.py:25
  28.3 6.8 %reshape.225 = bf16[3,9,16,65,16]{4,3,2,1,0:T(8,128)(2,1)} reshape(bf16[3,144,1040]{2,1,0:T(8,128)(2,1)S(1)} %pad_maximum_fusion) | data formatting | bytes 1797120 | tf_op jit(solution)/shard_map/reshape | solution.py:34
  35.0 7.2 %copy.53 = bf16[9,65,3,16,16]{1,4,3,2,0:T(8,128)(2,1)S(1)} copy(bf16[9,65,3,16,16]{4,1,3,0,2:T(8,128)(2,1)} %bitcast.68) | data formatting | bytes 1797120 | tf_op jit(solution)/shard_map/transpose | solution.py:35
  42.2 3.7 %fusion.58 = (bf16[8,64,768]{1,2,0:T(8,128)(2,1)}, bf16[8,64,768]{1,2,0:T(8,128)(2,1)}, bf16[8,64,768]{1,2,0:T(8,128)(2,1)}, bf16[8,64,768]{1,2,0:T(8,128)(2,1)}) fusion(bf16[9,65,768]{1,2,0:T(8,128)(2,1)S(1)} %bitcast.67), kind=kLoop, calls=%fused_computation.83 | loop fusion | bytes 6291456 | tf_op jit(solution)/shard_map/slice | solution.py:41
  45.9 1.8 copy.56
  47.7 1.4 copy.55
  49.1 3.8 %fusion.19 = f32[512,1024]{1,0:T(8,128)} fusion(bf16[512,768]{1,0:T(8,128)(2,1)S(1)} %bitcast.80, bf16[4,768,1024]{2,1,0:T(8,128)(2,1)} %param.9), kind=kOutput, calls=%fused_computation.26 | convolution fusion | flops 805306368 | bytes 4456448 | tf_op jit(solution)/shard_map/dot_general | solution.py:43
  52.9 3.8 %fusion.21 = f32[512,1024]{1,0:T(8,128)} fusion(bf16[512,768]{1,0:T(8,128)(2,1)S(1)} %bitcast.81, bf16[4,768,1024]{2,1,0:T(8,128)(2,1)} %param.9), kind=kOutput, calls=%fused_computation.28 | convolution fusion | flops 805306368 | bytes 4456448 | tf_op jit(solution)/shard_map/dot_general | solution.py:43
  56.7 0.7 copy.54
  57.4 3.9 %fusion.23 = f32[512,1024]{1,0:T(8,128)} fusion(bf16[512,768]{1,0:T(8,128)(2,1)S(1)} %bitcast.82, bf16[4,768,1024]{2,1,0:T(8,128)(2,1)} %param.9), kind=kOutput, calls=%fused_computation.30 | convolution fusion | flops 805306368 | bytes 4456448 | tf_op jit(solution)/shard_map/dot_general | solution.py:43
  61.3 0.7 copy.57
  61.9 4.4 %maximum_convert_fusion.1 = bf16[512,1024]{1,0:T(8,128)(2,1)S(1)} fusion(f32[512,1024]{1,0:T(8,128)} %fusion.19, f32[512,1024]{1,0:T(8,128)} %fusion.23, f32[512,1024]{1,0:T(8,128)} %fusion.21, bf16[512,768]{1,0:T(8,128)(2,1)S(1)} %bitcast.72, bf16[4,768,1024]{2,1,0:T(8,128)(2,1)} %param.9), kind=kOutput, calls=%fused_computation.21 | convolution fusion | flops 807927808 | bytes 9699328 | tf_op jit(solution)/shard_map/dot_general | solution.py:43
  66.3 2.9 %convolution_convert_fusion.1 = bf16[512,1024]{1,0:T(8,128)(2,1)S(1)} fusion(bf16[512,1024]{1,0:T(8,128)(2,1)S(1)} %copy-done, bf16[512,1024]{1,0:T(8,128)(2,1)S(1)} %maximum_convert_fusion.1, bf16[1024,512]{1,0:T(8,128)(2,1)} %param.10), kind=kOutput, calls=%fused_computation.37 | convolution fusion | flops 1074790400 | bytes 4194304 | tf_op jit(solution)/shard_map/dot_general | solution.py:77
  69.2 0.8 fusion.60
  70.1 0.8 slice.84
  71.4 0.7 gather_fusion
  73.2 24.3 %all-gather.5.cloned.1.call-done = bf16[32,64,256]{2,1,0:T(8,128)(2,1)} async-done(((bf16[8,64,256]{2,1,0:T(8,128)(2,1)}), bf16[32,64,256]{2,1,0:T(8,128)(2,1)}) %all-gather.5.cloned.1.call-update) | async-done | bytes 1048592 | tf_op jit(solution)/shard_map/all_gather | solution.py:87
  97.5 2.0 copy.59
  99.5 6.5 %copy.61 = bf16[32,64,8,32]{3,0,1,2:T(8,128)(2,1)} copy(bf16[32,64,8,32]{1,3,2,0:T(8,128)(2,1)S(1)} %bitcast.70) | data formatting | bytes 2097152 | tf_op jit(solution)/shard_map/reshape | solution.py:94
  106.0 4.7 %fusion.13 = (f32[8,64,8]{2,1,0:T(8,128)S(1)}, f32[8,64,8,32]{3,2,1,0:T(8,128)S(1)}) fusion(f32[8,8,32]{2,1,0:T(8,128)S(1)} %select_bitcast_fusion.1, bf16[8,64,8,32]{3,0,1,2:T(8,128)(2,1)S(1)} %copy.60, bf16[32,64,8,32]{3,0,1,2:T(8,128)(2,1)} %copy.61), kind=kOutput, calls=%fused_computation.22 | convolution fusion | flops 8777728 | bytes 1859584 | tf_op jit(solution)/shard_map/pwnd,ownd->nwpo/dot_general | solution.py:91
  110.8 1.3 fusion.16
  112.1 32.4 %all-gather.7.cloned.1.call-done = bf16[32,64,512]{2,1,0:T(8,128)(2,1)} async-done(((bf16[8,64,512]{2,1,0:T(8,128)(2,1)}), bf16[32,64,512]{2,1,0:T(8,128)(2,1)}) %all-gather.7.cloned.1.call-update) | async-done | bytes 2097168 | tf_op jit(solution)/shard_map/all_gather | solution.py:88
  144.5 6.2 %reshape.234 = bf16[32,64,8,64]{3,2,1,0:T(8,128)(2,1)} reshape(bf16[32,64,512]{2,1,0:T(8,128)(2,1)} %all-gather.7.cloned.1.call-done) | data formatting | bytes 4194304 | tf_op jit(solution)/shard_map/reshape | solution.py:107
  150.6 8.5 %fusion.8 = bf16[8,64,8,64]{3,0,1,2:T(8,128)(2,1)S(1)} fusion(bf16[32,64,8,64]{3,2,1,0:T(8,128)(2,1)} %reshape.234, f32[8,64,8,32]{3,2,1,0:T(8,128)S(1)} %get-tuple-element.18, f32[8,64,8]{0,1,2:T(8,128)S(1)} %bitcast.84, f32[8,64,8]{2,1,0:T(8,128)S(1)} %broadcast_maximum_fusion, f32[8,8,32]{2,1,0:T(8,128)S(1)} %select_bitcast_fusion.1), kind=kOutput, calls=%fused_computation.13 | convolution fusion | flops 17825792 | bytes 3186688 | tf_op jit(solution)/shard_map/nwpo,ownd->nwpd/dot_general | solution.py:54
  159.1 0.7 copy.65
  159.8 0.6 convert_element_type.41
  160.4 1.9 convolution_convert_fusion
  162.5 0.9 copy.79
  163.7 1.1 copy.80
  165.1 54.8 %gather_fusion.1 = f32[16384,8]{1,0:T(8,128)} fusion(f32[8,256]{0,1:T(8,128)S(1)} %copy.71, s32[16384]{0:T(1024)S(1)} %broadcast_clamp_fusion), kind=kCustom, calls=%fused_computation.1 | custom fusion | bytes 1114112 | tf_op jit(solution)/shard_map/jit(_take)/gather | solution.py:141
  219.9 5.2 %copy.72 = f32[64,256,8]{1,0,2:T(8,128)S(1)} copy(f32[64,256,8]{2,1,0:T(8,128)} %bitcast.69) | data formatting | bytes 1048576 | tf_op jit(solution)/shard_map/jit(_take)/gather | solution.py:141
  225.5 1.6 copy.68
  227.2 1.1 fusion.2
  228.3 1.9 copy-done.2
  230.2 1.5 fusion.3
  231.7 3.0 %copy.74 = bf16[8,256,512]{1,2,0:T(8,128)(2,1)S(1)} copy(bf16[8,256,512]{2,0,1:T(8,128)(2,1)} %all-gather.11.cloned.1.call-done) | data formatting | bytes 4194304 | tf_op jit(solution)/shard_map/all_gather | solution.py:126
  234.7 3.1 %fusion.36 = bf16[8,64,8,64]{3,1,0,2:T(8,128)(2,1)S(1)} fusion(f32[8,64,8]{1,0,2:T(8,128)S(1)} %bitcast.86, bf16[8,256,8,64]{1,3,2,0:T(8,128)(2,1)S(1)} %bitcast.75, f32[8,8,64,256]{3,2,1,0:T(8,128)} %copy-done.2, f32[8,8,64]{2,1,0:T(8,128)S(1)} %broadcast_maximum_fusion.1, f32[8,64,256]{2,1,0:T(8,128)S(1)} %select_bitcast_fusion), kind=kOutput, calls=%fused_computation.45 | convolution fusion | flops 139198464 | bytes 7372800 | tf_op jit(solution)/shard_map/nhwk,hknd->nhwd/dot_general | solution.py:54
  237.9 0.7 copy.76
  238.6 1.4 max.37
  240.0 3.1 %maximum_convert_fusion = bf16[512,1024]{1,0:T(8,128)(2,1)} fusion(bf16[512,1024]{1,0:T(8,128)(2,1)S(1)} %copy-done.7, bf16[512,512]{1,0:T(8,128)(2,1)} %max.37, bf16[512,1024]{1,0:T(8,128)(2,1)} %param.15), kind=kOutput, calls=%fused_computation.15 | convolution fusion | flops 538968064 | bytes 3670016 | tf_op jit(solution)/shard_map/dot_general | solution.py:151
  (56 shorter events, 3.5 us)
Async XLA Ops:
  6.5 59.8 %copy-start = (bf16[512,1024]{1,0:T(8,128)(2,1)S(1)}, bf16[512,1024]{1,0:T(8,128)(2,1)}, u32[]{:S(2)}) copy-start(bf16[512,1024]{1,0:T(8,128)(2,1)} %param.11) | copy-start | bytes 3145732
  6.5 90.9 %all-gather.5.cloned.1.call-start = ((), (), s32[]{:S(2)}) async-start(), calls=%async_computation | async-start | bytes 1310720 | tf_op jit(solution)/shard_map/all_gather | solution.py:87
  7.7 7.4 %collective-permute-start = (bf16[3,128,8]{2,1,0:T(8,128)(2,1)S(1)}, bf16[3,128,8]{2,1,0:T(8,128)(2,1)S(1)}, u32[]{:S(2)}, u32[]{:S(2)}) collective-permute-start(bf16[3,128,8]{2,1,0:T(8,128)(2,1)S(1)} %get-tuple-element.16), channel_id=1, source_target_pairs={{0,4},{4,8},{8,12},{12,0},{1,5},{5,9},{9,13},{13,1},{2,6},{6,10},{... | collective-permute-start | bytes 18440 | tf_op jit(solution)/shard_map/ppermute | solution.py:23
  10.7 6.1 %collective-permute-start.1 = (bf16[3,128,8]{2,1,0:T(8,128)(2,1)S(1)}, bf16[3,128,8]{2,1,0:T(8,128)(2,1)S(1)}, u32[]{:S(2)}, u32[]{:S(2)}) collective-permute-start(bf16[3,128,8]{2,1,0:T(8,128)(2,1)S(1)} %get-tuple-element.15), channel_id=1, source_target_pairs={{4,0},{8,4},{12,8},{0,12},{5,1},{9,5},{13,9},{1,13},{6,2},{10,6},{... | collective-permute-start | bytes 18440 | tf_op jit(solution)/shard_map/ppermute | solution.py:25
  18.6 5.3 %collective-permute-start.2 = (bf16[3,8,1040]{2,1,0:T(8,128)(2,1)S(1)}, bf16[3,8,1040]{2,1,0:T(8,128)(2,1)S(1)}, u32[]{:S(2)}, u32[]{:S(2)}) collective-permute-start(bf16[3,8,1040]{2,1,0:T(8,128)(2,1)S(1)} %get-tuple-element.13), channel_id=1, source_target_pairs={{0,1},{1,2},{2,3},{4,5},{5,6},{6,7},{8,9},{9,10},{10,11},{12,13},{... | collective-permute-start | bytes 149768 | tf_op jit(solution)/shard_map/ppermute | solution.py:23
  22.1 6.0 %collective-permute-start.3 = (bf16[3,8,1040]{2,1,0:T(8,128)(2,1)S(1)}, bf16[3,8,1040]{2,1,0:T(8,128)(2,1)S(1)}, u32[]{:S(2)}, u32[]{:S(2)}) collective-permute-start(bf16[3,8,1040]{2,1,0:T(8,128)(2,1)S(1)} %get-tuple-element.14), channel_id=1, source_target_pairs={{1,0},{2,1},{3,2},{5,4},{6,5},{7,6},{9,8},{10,9},{11,10},{13,12},{... | collective-permute-start | bytes 149768 | tf_op jit(solution)/shard_map/ppermute | solution.py:25
  45.9 1.9 copy-start.5
  49.1 3.8 %copy-start.8 = (bf16[8,64,768]{2,1,0:T(8,128)(2,1)S(1)}, bf16[8,64,768]{2,1,0:T(8,128)(2,1)}, u32[]{:S(2)}) copy-start(bf16[8,64,768]{2,1,0:T(8,128)(2,1)} %copy.55) | copy-start | bytes 2359300
  52.9 3.8 %copy-start.4 = (bf16[8,64,768]{1,2,0:T(8,128)(2,1)S(1)}, bf16[8,64,768]{1,2,0:T(8,128)(2,1)}, u32[]{:S(2)}) copy-start(bf16[8,64,768]{1,2,0:T(8,128)(2,1)} %get-tuple-element.8) | copy-start | bytes 2359300
  57.4 3.9 %copy-start.3 = (bf16[8,64,768]{1,2,0:T(8,128)(2,1)S(1)}, bf16[8,64,768]{1,2,0:T(8,128)(2,1)}, u32[]{:S(2)}) copy-start(bf16[8,64,768]{1,2,0:T(8,128)(2,1)} %get-tuple-element.5) | copy-start | bytes 2359300
  66.3 2.9 %copy-start.6 = (bf16[512,1024]{1,0:T(8,128)(2,1)}, bf16[512,1024]{1,0:T(8,128)(2,1)S(1)}, u32[]{:S(2)}) copy-start(bf16[512,1024]{1,0:T(8,128)(2,1)S(1)} %maximum_convert_fusion.1) | copy-start | bytes 3145732
  69.2 2.1 copy-start.10
  70.0 74.5 %all-gather.7.cloned.1.call-start = ((), (), s32[]{:S(2)}) async-start(), calls=%async_computation.1 | async-start | bytes 2621440 | tf_op jit(solution)/shard_map/all_gather | solution.py:88
  70.9 154.6 %all-gather.9.cloned.1.call-start = ((), (), s32[]{:S(2)}) async-start(), calls=%async_computation.2 | async-start | bytes 1310720 | tf_op jit(solution)/shard_map/all_gather | solution.py:125
  162.4 2.6 %copy-start.9 = (f32[8,256]{1,0:T(8,128)S(1)}, f32[8,256]{1,0:T(8,128)}, u32[]{:S(2)}) copy-start(f32[8,256]{1,0:T(8,128)} %param.14) | copy-start | bytes 24580
  163.3 68.4 %all-gather.11.cloned.1.call-start = ((), (), s32[]{:S(2)}) async-start(), calls=%async_computation.3 | async-start | bytes 2621440 | tf_op jit(solution)/shard_map/all_gather | solution.py:126
  228.3 1.9 copy-start.2
  237.9 2.2 copy-start.7
  238.6 4.5 %copy-start.1 = (bf16[512,1024]{1,0:T(8,128)(2,1)S(1)}, bf16[512,1024]{1,0:T(8,128)(2,1)}, u32[]{:S(2)}) copy-start(bf16[512,1024]{1,0:T(8,128)(2,1)} %param.11) | copy-start | bytes 3145732
Sparse Core Ops, SparseCore 0:
  70.1 27.2 all-gather.4
  99.0 45.3 all-gather.6
  163.5 25.3 all-gather.8
  190.6 35.2 all-gather.10
where the time goes:
time: 250 us
  local copies, waits for them, and re-layouts  116 us (46%)
  waiting for transfers between devices  66.6 us (27%)
  matrix products  41.2 us (16%)
  between operations  13.5 us (5%)
  starting transfers between devices  9.32 us (4%)
  other arithmetic  3.35 us (1%)
    gather x2, local copies, waits for them, and re-layouts, on_device(): scores = scores + jnp.take(width_bias, offsets, axis=1)[:, None]  59.9 us
    all_gather x1, waiting for transfers between devices, on_device(): lax.all_gather(height_proj[..., 2 * QK:], 'lat', axis=0, tiled=True)  32.4 us
    all_gather x1, waiting for transfers between devices, on_device(): lax.all_gather(height_proj[..., QK:2 * QK], 'lat', axis=0, tiled=True)  24.3 us
    dot_general x4, matrix products, stem_features(): jnp.dot(window, stem_weight[2 * row_shift + col_shift], preferred_element...  15.8 us
    dot_general x2, matrix products, online_update(): jnp.einsum(form, weights.astype(jnp.bfloat16), value_heads, preferred_ele...  11.6 us
    slice x5, local copies, waits for them, and re-layouts, stem_features(): blocks[row_shift:row_shift + map_rows, col_shift:col_shift + map_cols]  8.17 us
    transpose x1, local copies, waits for them, and re-layouts, stem_features(): blocks.transpose(1, 3, 0, 2, 4)  7.16 us
    reshape x1, local copies, waits for them, and re-layouts, stem_features(): blocks = padded.reshape(channels, map_rows + 1, PATCH, map_cols + 1, PATCH)  6.77 us
  transfers between devices with their start and end apart: 8, of which 6 were waited for; matrix products, arithmetic and copies ran while one was open for 33% of the time, Pallas kernels for 0%

commit v1 on v0

--- a/solution.py
+++ b/solution.py
@@ -10,6 +10,18 @@
 DQ = 32
 DV = 64
 lowest_score = -1e30
+
+
+def doubled_up(shard, axis, dim):
+    ways, here = (lax.axis_size(axis), lax.axis_index(axis))
+    grown, reach = (shard, 1)
+    while reach < ways:
+        theirs = lax.ppermute(grown, axis, [(d, d ^ reach) for d in range(ways)])
+        mine_first = jnp.concatenate([grown, theirs], axis=dim)
+        theirs_first = jnp.concatenate([theirs, grown], axis=dim)
+        grown = jnp.where(here & reach == 0, mine_first, theirs_first)
+        reach = 2 * reach
+    return grown
 
 
 def extended(cells, sides, width, closed):
@@ -85,7 +97,7 @@
         jnp.zeros((HEADS, map_cols, map_rows, DV), jnp.float32),
     )
     key_rows = lax.all_gather(height_proj[..., QK : 2 * QK], "lat", axis=0, tiled=True)
-    value_rows = lax.all_gather(height_proj[..., 2 * QK :], "lat", axis=0, tiled=True)
+    value_rows = doubled_up(height_proj[..., 2 * QK :], "lat", 0)
     key_count = key_rows.shape[0]
     scores = (
         jnp.einsum(

time: 250 us -> 264 us (1.056)
  other arithmetic: 3.35 us -> 11.7 us
  waiting for transfers between devices: 66.6 us -> 70.3 us
  starting transfers between devices: 9.32 us -> 12.8 us
  matrix products: 41.2 us -> 38.5 us
    ppermute x0 -> x2, waiting for transfers between devices: none -> 60.3 us  [doubled_up(): theirs = lax.ppermute(grown, axis, [(d, d ^ reach) for d in range(ways)])]
    all_gather x1 -> x0, waiting for transfers between devices: 32.4 us -> none  [on_device(): lax.all_gather(height_proj[..., 2 * QK:], 'lat', axis=0, tiled=True)]
    all_gather x1, waiting for transfers between devices: 24.3 us -> 0.01 us  [on_device(): lax.all_gather(height_proj[..., QK:2 * QK], 'lat', axis=0, tiled=True)]
    select_n x0 -> x3, other arithmetic: none -> 8.32 us  [doubled_up(): grown = jnp.where(here & reach == 0, mine_first, theirs_first)]
    concatenate x0 -> x3, local copies, waits for them, and re-layouts: none -> 6.95 us  [doubled_up(): mine_first = jnp.concatenate([grown, theirs], axis=dim)]
    reshape x1 -> x0, local copies, waits for them, and re-layouts: 6.17 us -> none  [on_device(): value_rows.reshape(key_count, map_cols, HEADS, DV)]
    ppermute x0 -> x2, starting transfers between devices: none -> 3.97 us  [doubled_up(): theirs = lax.ppermute(grown, axis, [(d, d ^ reach) for d in range(ways)])]
    dot_general x2, matrix products: 11.6 us -> 8.95 us  [online_update(): jnp.einsum(form, weights.astype(jnp.bfloat16), value_heads, preferred_ele...]
  transfers between devices with their start and end apart: 8 -> 9, of which waited for: 6 -> 6; matrix products, arithmetic and copies ran while one was open for 33% -> 32% of each run, Pallas kernels for 0% -> 0%
where the time goes in v1:
time: 264 us
  local copies, waits for them, and re-layouts  117 us (44%)
  waiting for transfers between devices  70.3 us (27%)
  matrix products  38.5 us (15%)
  between operations  13.5 us (5%)
  starting transfers between devices  12.8 us (5%)
  other arithmetic  11.7 us (4%)
    ppermute x2, waiting for transfers between devices, doubled_up(): theirs = lax.ppermute(grown, axis, [(d, d ^ reach) for d in range(ways)])  60.3 us
    gather x2, local copies, waits for them, and re-layouts, on_device(): scores = scores + jnp.take(width_bias, offsets, axis=1)[:, None]  60.1 us
    dot_general x4, matrix products, stem_features(): jnp.dot(window, stem_weight[2 * row_shift + col_shift], preferred_element...  15.8 us
    dot_general x2, matrix products, online_update(): jnp.einsum(form, weights.astype(jnp.bfloat16), value_heads, preferred_ele...  8.95 us
    select_n x3, other arithmetic, doubled_up(): grown = jnp.where(here & reach == 0, mine_first, theirs_first)  8.32 us
    slice x5, local copies, waits for them, and re-layouts, stem_features(): blocks[row_shift:row_shift + map_rows, col_shift:col_shift + map_cols]  8.14 us
    transpose x1, local copies, waits for them, and re-layouts, stem_features(): blocks.transpose(1, 3, 0, 2, 4)  7.16 us
    concatenate x3, local copies, waits for them, and re-layouts, doubled_up(): mine_first = jnp.concatenate([grown, theirs], axis=dim)  6.95 us
  transfers between devices with their start and end apart: 9, of which 6 were waited for; matrix products, arithmetic and copies ran while one was open for 32% of the time, Pallas kernels for 0%

profile of v1, /device:TPU:0, one launch (start us, length us, event | category | flops | bytes accessed | tf_op | source)
XLA Modules:
  0.0 263.7 jit_solution(10256018806202555361)
XLA Ops:
  6.5 1.1 fusion.62
  7.7 3.0 %collective-permute-start = (bf16[3,128,8]{2,1,0:T(8,128)(2,1)S(1)}, bf16[3,128,8]{2,1,0:T(8,128)(2,1)S(1)}, u32[]{:S(2)}, u32[]{:S(2)}) collective-permute-start(bf16[3,128,8]{2,1,0:T(8,128)(2,1)S(1)} %get-tuple-element.16), channel_id=1, source_target_pairs={{0,4},{4,8},{8,12},{12,0},{1,5},{5,9},{9,13},{13,1},{2,6},{6,10},{... | collective-permute-start | bytes 18440 | tf_op jit(solution)/shard_map/ppermute | solution.py:35
  10.7 1.0 collective-permute-start.1
  11.7 3.4 %collective-permute-done = bf16[3,128,8]{2,1,0:T(8,128)(2,1)S(1)} collective-permute-done((bf16[3,128,8]{2,1,0:T(8,128)(2,1)S(1)}, bf16[3,128,8]{2,1,0:T(8,128)(2,1)S(1)}, u32[]{:S(2)}, u32[]{:S(2)}) %collective-permute-start) | collective-permute-done | bytes 6176 | tf_op jit(solution)/shard_map/ppermute | solution.py:35
  15.1 1.7 collective-permute-done.1
  16.8 1.8 concatenate.32
  18.6 3.5 %collective-permute-start.2 = (bf16[3,8,1040]{2,1,0:T(8,128)(2,1)S(1)}, bf16[3,8,1040]{2,1,0:T(8,128)(2,1)S(1)}, u32[]{:S(2)}, u32[]{:S(2)}) collective-permute-start(bf16[3,8,1040]{2,1,0:T(8,128)(2,1)S(1)} %get-tuple-element.13), channel_id=1, source_target_pairs={{0,1},{1,2},{2,3},{4,5},{5,6},{6,7},{8,9},{9,10},{10,11},{12,13},{... | collective-permute-start | bytes 149768 | tf_op jit(solution)/shard_map/ppermute | solution.py:35
  22.1 1.3 collective-permute-start.3
  23.9 4.3 %collective-permute-done.3 = bf16[3,8,1040]{2,1,0:T(8,128)(2,1)S(1)} collective-permute-done((bf16[3,8,1040]{2,1,0:T(8,128)(2,1)S(1)}, bf16[3,8,1040]{2,1,0:T(8,128)(2,1)S(1)}, u32[]{:S(2)}, u32[]{:S(2)}) %collective-permute-start.3) | collective-permute-done | bytes 49952 | tf_op jit(solution)/shard_map/ppermute | solution.py:37
  28.3 6.8 %reshape.231 = bf16[3,9,16,65,16]{4,3,2,1,0:T(8,128)(2,1)} reshape(bf16[3,144,1040]{2,1,0:T(8,128)(2,1)S(1)} %pad_maximum_fusion) | data formatting | bytes 1797120 | tf_op jit(solution)/shard_map/reshape | solution.py:46
  35.0 7.2 %copy.53 = bf16[9,65,3,16,16]{1,4,3,2,0:T(8,128)(2,1)S(1)} copy(bf16[9,65,3,16,16]{4,1,3,0,2:T(8,128)(2,1)} %bitcast.68) | data formatting | bytes 1797120 | tf_op jit(solution)/shard_map/transpose | solution.py:47
  42.2 3.6 %fusion.58 = (bf16[8,64,768]{1,2,0:T(8,128)(2,1)}, bf16[8,64,768]{1,2,0:T(8,128)(2,1)}, bf16[8,64,768]{1,2,0:T(8,128)(2,1)}, bf16[8,64,768]{1,2,0:T(8,128)(2,1)}) fusion(bf16[9,65,768]{1,2,0:T(8,128)(2,1)S(1)} %bitcast.67), kind=kLoop, calls=%fused_computation.86 | loop fusion | bytes 6291456 | tf_op jit(solution)/shard_map/slice | solution.py:53
  45.8 1.8 copy.56
  47.7 1.4 copy.55
  49.1 3.8 %fusion.19 = f32[512,1024]{1,0:T(8,128)} fusion(bf16[512,768]{1,0:T(8,128)(2,1)S(1)} %bitcast.80, bf16[4,768,1024]{2,1,0:T(8,128)(2,1)} %param.9), kind=kOutput, calls=%fused_computation.28 | convolution fusion | flops 805306368 | bytes 4456448 | tf_op jit(solution)/shard_map/dot_general | solution.py:55
  52.9 3.8 %fusion.21 = f32[512,1024]{1,0:T(8,128)} fusion(bf16[512,768]{1,0:T(8,128)(2,1)S(1)} %bitcast.81, bf16[4,768,1024]{2,1,0:T(8,128)(2,1)} %param.9), kind=kOutput, calls=%fused_computation.30 | convolution fusion | flops 805306368 | bytes 4456448 | tf_op jit(solution)/shard_map/dot_general | solution.py:55
  57.4 3.8 %fusion.23 = f32[512,1024]{1,0:T(8,128)} fusion(bf16[512,768]{1,0:T(8,128)(2,1)S(1)} %bitcast.82, bf16[4,768,1024]{2,1,0:T(8,128)(2,1)} %param.9), kind=kOutput, calls=%fused_computation.32 | convolution fusion | flops 805306368 | bytes 4456448 | tf_op jit(solution)/shard_map/dot_general | solution.py:55
  61.9 4.4 %maximum_convert_fusion.1 = bf16[512,1024]{1,0:T(8,128)(2,1)S(1)} fusion(f32[512,1024]{1,0:T(8,128)} %fusion.19, f32[512,1024]{1,0:T(8,128)} %fusion.23, f32[512,1024]{1,0:T(8,128)} %fusion.21, bf16[512,768]{1,0:T(8,128)(2,1)S(1)} %bitcast.72, bf16[4,768,1024]{2,1,0:T(8,128)(2,1)} %param.9), kind=kOutput, calls=%fused_computation.23 | convolution fusion | flops 807927808 | bytes 9699328 | tf_op jit(solution)/shard_map/dot_general | solution.py:55
  66.3 2.9 %convolution_convert_fusion.1 = bf16[512,1024]{1,0:T(8,128)(2,1)S(1)} fusion(bf16[512,1024]{1,0:T(8,128)(2,1)S(1)} %copy-done, bf16[512,1024]{1,0:T(8,128)(2,1)S(1)} %maximum_convert_fusion.1, bf16[1024,512]{1,0:T(8,128)(2,1)} %param.10), kind=kOutput, calls=%fused_computation.39 | convolution fusion | flops 1074790400 | bytes 4194304 | tf_op jit(solution)/shard_map/dot_general | solution.py:89
  69.2 1.6 collective-permute-start.4
  71.7 9.2 %collective-permute-done.4 = bf16[8,64,512]{2,1,0:T(8,128)(2,1)S(1)} collective-permute-done((bf16[8,64,512]{2,1,0:T(8,128)(2,1)S(1)}, bf16[8,64,512]{2,1,0:T(8,128)(2,1)S(1)}, u32[]{:S(2)}, u32[]{:S(2)}) %collective-permute-start.4) | collective-permute-done | bytes 524320 | tf_op jit(solution)/shard_map/ppermute | solution.py:19
  80.9 1.2 maximum_select_fusion.2
  82.1 2.3 collective-permute-start.5
  85.6 1.5 concatenate.34
  87.4 1.6 copy.60
  89.0 1.5 concatenate.35
  90.5 2.4 maximum_select_fusion.1
  92.9 51.2 %collective-permute-done.5 = bf16[16,64,512]{2,1,0:T(8,128)(2,1)} collective-permute-done((bf16[16,64,512]{2,1,0:T(8,128)(2,1)}, bf16[16,64,512]{2,1,0:T(8,128)(2,1)}, u32[]{:S(2)}, u32[]{:S(2)}) %collective-permute-start.5) | collective-permute-done | bytes 1048608 | tf_op jit(solution)/shard_map/ppermute | solution.py:19
  144.1 3.9 %concatenate.40 = bf16[16,64,8,64]{3,2,1,0:T(8,128)(2,1)} reshape(bf16[16,64,512]{2,1,0:T(8,128)(2,1)} %collective-permute-done.5) | data formatting | bytes 2097152 | tf_op jit(solution)/shard_map/concatenate | solution.py:20
  148.0 4.7 %maximum_select_fusion = bf16[32,64,8,64]{3,2,1,0:T(8,128)(2,1)} fusion(bf16[16,64,8,64]{3,2,1,0:T(8,128)(2,1)} %concatenate.40, bf16[16,64,8,64]{3,2,1,0:T(8,128)(2,1)S(1)} %maximum_select_fusion.1, pred[]{:T(512)S(6)} %eq.8), kind=kLoop, calls=%fused_computation.2 | loop fusion | flops 3145728 | bytes 4194305 | tf_op jit(solution)/shard_map/jit(_where)/select_n | solution.py:22
  152.7 2.0 copy.59
  154.8 6.6 %copy.61 = bf16[32,64,8,32]{3,0,1,2:T(8,128)(2,1)} copy(bf16[32,64,8,32]{1,3,2,0:T(8,128)(2,1)S(1)} %bitcast.70) | data formatting | bytes 2097152 | tf_op jit(solution)/shard_map/reshape | solution.py:106
  161.3 4.7 %fusion.13 = (f32[8,64,8]{2,1,0:T(8,128)S(1)}, f32[8,64,8,32]{3,2,1,0:T(8,128)S(1)}) fusion(f32[8,8,32]{2,1,0:T(8,128)S(1)} %select_bitcast_fusion.1, bf16[8,64,8,32]{3,0,1,2:T(8,128)(2,1)S(1)} %copy-done.8, bf16[32,64,8,32]{3,0,1,2:T(8,128)(2,1)} %copy.61), kind=kOutput, calls=%fused_computation.24 | convolution fusion | flops 8777728 | bytes 1859584 | tf_op jit(solution)/shard_map/pwnd,ownd->nwpo/dot_general | solution.py:103
  166.1 1.3 fusion.16
  167.4 5.8 %fusion.8 = bf16[8,64,8,64]{3,0,1,2:T(8,128)(2,1)S(1)} fusion(bf16[32,64,8,64]{3,2,1,0:T(8,128)(2,1)S(1)} %copy-done.7, f32[8,64,8,32]{3,2,1,0:T(8,128)S(1)} %get-tuple-element.18, f32[8,64,8]{0,1,2:T(8,128)S(1)} %bitcast.84, f32[8,64,8]{2,1,0:T(8,128)S(1)} %broadcast_maximum_fusion, f32[8,8,32]{2,1,0:T(8,128)S(1)} %select_bitcast_fusion.1), kind=kOutput, calls=%fused_computation.15 | convolution fusion | flops 17825792 | bytes 3186688 | tf_op jit(solution)/shard_map/nwpo,ownd->nwpd/dot_general | solution.py:66
  174.5 1.9 convolution_convert_fusion
  176.5 0.9 copy.79
  177.5 1.1 copy.80
  179.0 55.0 %gather_fusion.1 = f32[16384,8]{1,0:T(8,128)} fusion(f32[8,256]{0,1:T(8,128)S(1)} %copy.71, s32[16384]{0:T(1024)S(1)} %broadcast_clamp_fusion), kind=kCustom, calls=%fused_computation.1 | custom fusion | bytes 1114112 | tf_op jit(solution)/shard_map/jit(_take)/gather | solution.py:153
  233.9 5.2 %copy.72 = f32[64,256,8]{1,0,2:T(8,128)S(1)} copy(f32[64,256,8]{2,1,0:T(8,128)} %bitcast.69) | data formatting | bytes 1048576 | tf_op jit(solution)/shard_map/jit(_take)/gather | solution.py:153
  239.6 1.6 copy.68
  241.2 1.1 fusion.2
  242.3 1.9 copy-done.2
  244.3 1.5 fusion.3
  245.8 3.0 %copy.74 = bf16[8,256,512]{1,2,0:T(8,128)(2,1)S(1)} copy(bf16[8,256,512]{2,0,1:T(8,128)(2,1)} %all-gather.8.cloned.1.call-done) | data formatting | bytes 4194304 | tf_op jit(solution)/shard_map/all_gather | solution.py:138
  248.8 3.1 %fusion.36 = bf16[8,64,8,64]{3,1,0,2:T(8,128)(2,1)S(1)} fusion(f32[8,64,8]{1,0,2:T(8,128)S(1)} %bitcast.86, bf16[8,256,8,64]{1,3,2,0:T(8,128)(2,1)S(1)} %bitcast.75, f32[8,8,64,256]{3,2,1,0:T(8,128)} %copy-done.2, f32[8,8,64]{2,1,0:T(8,128)S(1)} %broadcast_maximum_fusion.1, f32[8,64,256]{2,1,0:T(8,128)S(1)} %select_bitcast_fusion), kind=kOutput, calls=%fused_computation.48 | convolution fusion | flops 139198464 | bytes 7372800 | tf_op jit(solution)/shard_map/nhwk,hknd->nhwd/dot_general | solution.py:66
  252.7 1.4 max.37
  254.1 3.1 %maximum_convert_fusion = bf16[512,1024]{1,0:T(8,128)(2,1)} fusion(bf16[512,1024]{1,0:T(8,128)(2,1)S(1)} %copy-done.10, bf16[512,512]{1,0:T(8,128)(2,1)} %max.37, bf16[512,1024]{1,0:T(8,128)(2,1)} %param.15), kind=kOutput, calls=%fused_computation.17 | convolution fusion | flops 538968064 | bytes 3670016 | tf_op jit(solution)/shard_map/dot_general | solution.py:163
  (68 shorter events, 7.3 us)
Async XLA Ops:
  6.5 59.8 %copy-start = (bf16[512,1024]{1,0:T(8,128)(2,1)S(1)}, bf16[512,1024]{1,0:T(8,128)(2,1)}, u32[]{:S(2)}) copy-start(bf16[512,1024]{1,0:T(8,128)(2,1)} %param.11) | copy-start | bytes 3145732
  6.5 146.2 %all-gather.4.cloned.1.call-start = ((), (), s32[]{:S(2)}) async-start(), calls=%async_computation | async-start | bytes 1310720 | tf_op jit(solution)/shard_map/all_gather | solution.py:99
  7.7 7.4 %collective-permute-start = (bf16[3,128,8]{2,1,0:T(8,128)(2,1)S(1)}, bf16[3,128,8]{2,1,0:T(8,128)(2,1)S(1)}, u32[]{:S(2)}, u32[]{:S(2)}) collective-permute-start(bf16[3,128,8]{2,1,0:T(8,128)(2,1)S(1)} %get-tuple-element.16), channel_id=1, source_target_pairs={{0,4},{4,8},{8,12},{12,0},{1,5},{5,9},{9,13},{13,1},{2,6},{6,10},{... | collective-permute-start | bytes 18440 | tf_op jit(solution)/shard_map/ppermute | solution.py:35
  10.7 6.1 %collective-permute-start.1 = (bf16[3,128,8]{2,1,0:T(8,128)(2,1)S(1)}, bf16[3,128,8]{2,1,0:T(8,128)(2,1)S(1)}, u32[]{:S(2)}, u32[]{:S(2)}) collective-permute-start(bf16[3,128,8]{2,1,0:T(8,128)(2,1)S(1)} %get-tuple-element.15), channel_id=1, source_target_pairs={{4,0},{8,4},{12,8},{0,12},{5,1},{9,5},{13,9},{1,13},{6,2},{10,6},{... | collective-permute-start | bytes 18440 | tf_op jit(solution)/shard_map/ppermute | solution.py:37
  18.6 5.3 %collective-permute-start.2 = (bf16[3,8,1040]{2,1,0:T(8,128)(2,1)S(1)}, bf16[3,8,1040]{2,1,0:T(8,128)(2,1)S(1)}, u32[]{:S(2)}, u32[]{:S(2)}) collective-permute-start(bf16[3,8,1040]{2,1,0:T(8,128)(2,1)S(1)} %get-tuple-element.13), channel_id=1, source_target_pairs={{0,1},{1,2},{2,3},{4,5},{5,6},{6,7},{8,9},{9,10},{10,11},{12,13},{... | collective-permute-start | bytes 149768 | tf_op jit(solution)/shard_map/ppermute | solution.py:35
  22.1 6.0 %collective-permute-start.3 = (bf16[3,8,1040]{2,1,0:T(8,128)(2,1)S(1)}, bf16[3,8,1040]{2,1,0:T(8,128)(2,1)S(1)}, u32[]{:S(2)}, u32[]{:S(2)}) collective-permute-start(bf16[3,8,1040]{2,1,0:T(8,128)(2,1)S(1)} %get-tuple-element.14), channel_id=1, source_target_pairs={{1,0},{2,1},{3,2},{5,4},{6,5},{7,6},{9,8},{10,9},{11,10},{13,12},{... | collective-permute-start | bytes 149768 | tf_op jit(solution)/shard_map/ppermute | solution.py:37
  45.8 1.9 copy-start.5
  49.1 3.8 %copy-start.11 = (bf16[8,64,768]{2,1,0:T(8,128)(2,1)S(1)}, bf16[8,64,768]{2,1,0:T(8,128)(2,1)}, u32[]{:S(2)}) copy-start(bf16[8,64,768]{2,1,0:T(8,128)(2,1)} %copy.55) | copy-start | bytes 2359300
  52.9 3.8 %copy-start.4 = (bf16[8,64,768]{1,2,0:T(8,128)(2,1)S(1)}, bf16[8,64,768]{1,2,0:T(8,128)(2,1)}, u32[]{:S(2)}) copy-start(bf16[8,64,768]{1,2,0:T(8,128)(2,1)} %get-tuple-element.8) | copy-start | bytes 2359300
  57.4 3.9 %copy-start.3 = (bf16[8,64,768]{1,2,0:T(8,128)(2,1)S(1)}, bf16[8,64,768]{1,2,0:T(8,128)(2,1)}, u32[]{:S(2)}) copy-start(bf16[8,64,768]{1,2,0:T(8,128)(2,1)} %get-tuple-element.5) | copy-start | bytes 2359300
  66.3 2.9 %copy-start.9 = (bf16[512,1024]{1,0:T(8,128)(2,1)}, bf16[512,1024]{1,0:T(8,128)(2,1)S(1)}, u32[]{:S(2)}) copy-start(bf16[512,1024]{1,0:T(8,128)(2,1)S(1)} %maximum_convert_fusion.1) | copy-start | bytes 3145732
  69.2 15.4 %copy-start.13 = (f32[8,63]{1,0:T(8,128)S(1)}, f32[8,63]{1,0:T(8,128)}, u32[]{:S(2)}) copy-start(f32[8,63]{1,0:T(8,128)} %param.12) | copy-start | bytes 6052
  69.2 11.7 %collective-permute-start.4 = (bf16[8,64,512]{2,1,0:T(8,128)(2,1)S(1)}, bf16[8,64,512]{2,1,0:T(8,128)(2,1)S(1)}, u32[]{:S(2)}, u32[]{:S(2)}) collective-permute-start(bf16[8,64,512]{2,1,0:T(8,128)(2,1)S(1)} %slice.84), channel_id=1, source_target_pairs={{0,1},{1,0},{2,3},{3,2},{4,5},{5,4},{6,7},{7,6},{8,9},{9,8},{10,11... | collective-permute-start | bytes 1572872 | tf_op jit(solution)/shard_map/ppermute | solution.py:19
  71.7 167.9 %all-gather.6.cloned.1.call-start = ((), (), s32[]{:S(2)}) async-start(), calls=%async_computation.1 | async-start | bytes 1310720 | tf_op jit(solution)/shard_map/all_gather | solution.py:137
  82.1 62.0 %collective-permute-start.5 = (bf16[16,64,512]{2,1,0:T(8,128)(2,1)}, bf16[16,64,512]{2,1,0:T(8,128)(2,1)}, u32[]{:S(2)}, u32[]{:S(2)}) collective-permute-start(bf16[16,64,512]{2,1,0:T(8,128)(2,1)} %maximum_select_fusion.2), channel_id=1, source_target_pairs={{0,2},{1,3},{2,0},{3,1},{4,6},{5,7},{6,4},{7,5},{8,10},{9,11},{10,... | collective-permute-start | bytes 3145736 | tf_op jit(solution)/shard_map/ppermute | solution.py:19
  87.1 3.4 %copy-start.6 = (bf16[8,64,8,64]{3,2,1,0:T(8,128)(2,1)S(1)}, bf16[8,64,8,64]{3,2,1,0:T(8,128)(2,1)}, u32[]{:S(2)}) copy-start(bf16[8,64,8,64]{3,2,1,0:T(8,128)(2,1)} %concatenate.34) | copy-start | bytes 1572868
  154.7 6.6 %copy-start.8 = (bf16[8,64,8,32]{3,0,1,2:T(8,128)(2,1)S(1)}, bf16[8,64,8,32]{3,0,1,2:T(8,128)(2,1)}, u32[]{:S(2)}) copy-start(bf16[8,64,8,32]{3,0,1,2:T(8,128)(2,1)} %copy.60) | copy-start | bytes 786436
  161.3 6.1 %copy-start.7 = (bf16[32,64,8,64]{3,2,1,0:T(8,128)(2,1)S(1)}, bf16[32,64,8,64]{3,2,1,0:T(8,128)(2,1)}, u32[]{:S(2)}) copy-start(bf16[32,64,8,64]{3,2,1,0:T(8,128)(2,1)} %maximum_select_fusion) | copy-start | bytes 6291460
  176.5 2.3 copy-start.12
  177.4 68.4 %all-gather.8.cloned.1.call-start = ((), (), s32[]{:S(2)}) async-start(), calls=%async_computation.2 | async-start | bytes 2621440 | tf_op jit(solution)/shard_map/all_gather | solution.py:138
  242.3 1.9 copy-start.2
  251.9 2.2 copy-start.10
  252.7 4.5 %copy-start.1 = (bf16[512,1024]{1,0:T(8,128)(2,1)S(1)}, bf16[512,1024]{1,0:T(8,128)(2,1)}, u32[]{:S(2)}) copy-start(bf16[512,1024]{1,0:T(8,128)(2,1)} %param.11) | copy-start | bytes 3145732
Sparse Core Ops, SparseCore 0:
  71.8 58.1 all-gather.3
  177.5 25.6 all-gather.5
  205.1 35.2 all-gather.7
